TPU v7x, 128 devices: a whole 4x4x4 slice. The times are simulated.
128 devices in a mesh: dp: 32 (over y, z, core), vocab: 4 (over x).
Axes of the slice: x: 4, y: 4, z: 4, core: 2. Of those that a mesh axis runs over, the one named last changes fastest.
Arguments:
- token_grads: bfloat16 [32768, 5376], P(('dp', 'vocab')), may hold values from -24 to 24
- row_holder: int32 [32768, 1], P(('dp', 'vocab')), may hold values from 0 to 127; in each aligned block of 256 rows (0 to 255, 256 to 511, ...) at most 3 rows name the same one
- row_offset: int32 [32768], P(('dp', 'vocab')), may hold values from 0 to 255
- table: bfloat16 [32768, 5376], P(('dp', 'vocab')), may hold values from -6 to 6
- first_moment: bfloat16 [32768, 5376], P(('dp', 'vocab')), may hold values from -3 to 3
- second_moment: bfloat16 [32768, 5376], P(('dp', 'vocab')), may hold values from 0.049804688 to 4
Outputs:
- new_table: bfloat16 [32768, 5376], P(('dp', 'vocab'))
- new_first: bfloat16 [32768, 5376], P(('dp', 'vocab'))
- new_second: bfloat16 [32768, 5376], P(('dp', 'vocab'))
Inputs may be any that keep to these rules, and one draw needn't show every extreme that they name: `row_holder`: among the tokens of one device, at most 3 name the same holder, and some device has a holder named exactly 3 times.
All inputs are finite; a program needn't handle non-finite values.
Results may differ from a plain program's by a relative error of at most 0.0004.
Values may be sent and summed in bfloat16 or wider, within the bound.
No kernel may reach another device: no remote copies, remote signals or barrier semaphores. Data moves between devices by JAX's collectives and lax.ppermute only.
A program may use at most 128 MiB of HBM per device.

v0:
```python
import jax
import jax.numpy as jnp
from jax import lax
from jax.sharding import PartitionSpec as P


def body(token_grads, row_holder, row_offset, table, first_moment, second_moment):
    n_data = lax.axis_size("dp")
    n_owner = lax.axis_size("vocab")
    devices = n_data * n_owner
    tok_count = token_grads.shape[0]
    width = token_grads.shape[1]
    rows_here = table.shape[0]
    capacity = max(2, 3 * tok_count // (2 * devices))
    destination = row_holder[:, 0]
    one_hot = (destination[:, None] == jnp.arange(devices, dtype=jnp.int32)[None, :]).astype(
        jnp.int32
    )
    earlier = jnp.cumsum(one_hot, axis=0) - one_hot
    slot_rank = jnp.sum(earlier * one_hot, axis=1)
    position = destination * capacity + slot_rank
    outgoing = jnp.zeros((devices * capacity, width), jnp.bfloat16).at[position].set(token_grads)
    targets = (
        jnp.full((devices * capacity,), -1.0, jnp.bfloat16)
        .at[position]
        .set(row_offset.astype(jnp.bfloat16))
    )
    arrived, arrived_targets = (
        lax.all_to_all(outgoing, ("dp", "vocab"), split_axis=0, concat_axis=0, tiled=True),
        lax.all_to_all(targets, ("dp", "vocab"), split_axis=0, concat_axis=0, tiled=True),
    )
    incidence = (
        jnp.arange(rows_here, dtype=jnp.int32)[:, None]
        == arrived_targets.astype(jnp.int32)[None, :]
    ).astype(jnp.bfloat16)
    grad_sum = jnp.dot(incidence, arrived, preferred_element_type=jnp.float32)
    total = lax.psum(jnp.sum(grad_sum * grad_sum), ("dp", "vocab"))
    limit = 2.0 * jnp.sqrt(jnp.float32(tok_count * devices * width))
    factor = jnp.minimum(jnp.float32(1.0), limit / jnp.sqrt(total))
    grad = factor * grad_sum
    first = 0.9 * first_moment.astype(jnp.float32) + 0.1 * grad
    second = 0.95 * second_moment.astype(jnp.float32) + 0.05 * grad * grad
    step_size = first / (1.0 - 0.9**10) / (jnp.sqrt(second / (1.0 - 0.95**10)) + 1e-08)
    new_table = (table.astype(jnp.float32) - 0.02 * step_size).astype(jnp.bfloat16)
    return (new_table, first.astype(jnp.bfloat16), second.astype(jnp.bfloat16))


def solution(mesh):
    placed = (
        P(("dp", "vocab"), None),
        P(("dp", "vocab"), None),
        P(("dp", "vocab")),
        P(("dp", "vocab"), None),
        P(("dp", "vocab"), None),
        P(("dp", "vocab"), None),
    )
    return jax.shard_map(
        body,
        mesh=mesh,
        in_specs=placed,
        out_specs=(P(("dp", "vocab"), None), P(("dp", "vocab"), None), P(("dp", "vocab"), None)),
        check_vma=False,
    )
```

profile of v0, /device:TPU:1, one launch (start us, length us, event | category | flops | bytes accessed | tf_op | source)
XLA Modules:
  0.0 201.1 jit_solution(10168442971995907120)
XLA Ops:
  0.6 0.7 convert_element_type.43
  1.3 0.8 copy.12
  2.1 0.2 fusion.7
  2.4 0.9 fusion.9
  3.3 0.7 compare_select_fusion
  4.0 2.2 %scatter_custom_fusion = bf16[384]{0:T(512)(128)(2,1)S(1)} fusion(s32[256]{0:T(256)S(1)} %bitcast.26, bf16[256]{0:T(256)(128)(2,1)S(1)} %convert_element_type.43, bf16[]{:T(256)} %constant.5.clone.1), kind=kCustom, calls=%fused_computation.26 | custom fusion | bytes 770 | tf_op jit(solution)/shard_map/scatter | solution.py:26
  6.1 0.9 all_to_all.19
  7.0 11.5 %all-to-all-start = ((bf16[128,3,1]{1,2,0:T(2,128)(2,1)}), bf16[128,3,1]{1,2,0:T(2,128)(2,1)S(1)}, u32[]{:S(2)}, u32[]{:S(2)}) async-start(bf16[128,3,1]{1,2,0:T(2,128)(2,1)} %all_to_all.19), calls=%async_computation | async-start | bytes 131072 | tf_op jit(solution)/shard_map/all_to_all | solution.py:30
  18.5 8.0 %scatter_custom_fusion.1 = bf16[384,5376]{1,0:T(8,128)(2,1)} fusion(s32[256]{0:T(256)S(1)} %bitcast.27, bf16[256,5376]{1,0:T(8,128)(2,1)} %param.6, bf16[]{:T(256)} %constant.9.clone.1), kind=kCustom, calls=%fused_computation.9 | custom fusion | bytes 4129280 | tf_op jit(solution)/shard_map/scatter | solution.py:22
  26.5 7.6 %all_to_all.16 = bf16[128,3,5376]{2,1,0:T(4,128)(2,1)} reshape(bf16[384,5376]{1,0:T(8,128)(2,1)} %scatter_custom_fusion.1) | data formatting | bytes 8257536 | tf_op jit(solution)/shard_map/all_to_all | solution.py:29
  34.0 0.0 all-to-all-done
  34.0 10.2 %all-to-all-start.1 = ((bf16[128,3,5376]{2,1,0:T(4,128)(2,1)}), bf16[128,3,5376]{2,1,0:T(4,128)(2,1)}, u32[]{:S(2)}, u32[]{:S(2)}) async-start(bf16[128,3,5376]{2,1,0:T(4,128)(2,1)} %all_to_all.16), calls=%async_computation.1 | async-start | bytes 11010048 | tf_op jit(solution)/shard_map/all_to_all | solution.py:29
  44.2 0.2 convert_reduce_fusion
  44.4 0.2 reshape.35
  44.6 66.8 %all-to-all-done.1 = bf16[128,3,5376]{2,1,0:T(4,128)(2,1)} async-done(((bf16[128,3,5376]{2,1,0:T(4,128)(2,1)}), bf16[128,3,5376]{2,1,0:T(4,128)(2,1)}, u32[]{:S(2)}, u32[]{:S(2)}) %all-to-all-start.1) | async-done | bytes 4128800 | tf_op jit(solution)/shard_map/all_to_all | solution.py:29
  111.5 8.3 %all_to_all.18 = bf16[384,5376]{1,0:T(8,128)(2,1)} reshape(bf16[128,3,5376]{2,1,0:T(4,128)(2,1)} %all-to-all-done.1) | data formatting | bytes 8257536 | tf_op jit(solution)/shard_map/all_to_all | solution.py:29
  119.8 0.0 copy-start
  119.8 6.9 %multiply_reduce_fusion = (f32[]{:T(128)}, f32[256,5376]{1,0:T(8,128)}) fusion(bf16[384,5376]{1,0:T(8,128)(2,1)} %all_to_all.18, s32[384]{0:T(512)S(1)} %reshape.35), kind=kOutput, calls=%fused_computation.6 | convolution fusion | flops 1059815424 | bytes 9635332 | tf_op jit(solution)/shard_map/dot_general | solution.py:36
  126.7 62.9 %psum.7 = f32[]{:T(128)} all-reduce(f32[]{:T(128)} %get-tuple-element.6), channel_id=1, replica_groups=mesh['dp'=32,'vocab'=4] {'dp','vocab'}, use_global_device_ids=true, to_apply=%region_6.7 | all-reduce | flops 1 | bytes 8 | tf_op jit(solution)/shard_map/psum | solution.py:37
  190.3 0.0 copy-done
  190.3 10.8 %fusion.2 = (bf16[256,5376]{1,0:T(8,128)(2,1)}, bf16[256,5376]{1,0:T(8,128)(2,1)}, bf16[256,5376]{1,0:T(8,128)(2,1)}) fusion(f32[256,5376]{1,0:T(8,128)} %get-tuple-element.7, bf16[256,5376]{1,0:T(8,128)(2,1)S(1)} %copy-done, f32[]{:T(128)S(6)} %min_shard_map.3, bf16[256,5376]{1,0:T(8,128)(2,1)} %param.10, bf16[256,5376]{1,0:T(8,128)(2,1)} %param.9), kind=kLoop, calls=%fused_computation.8 | loop fusion | flops 27525120 | bytes 22020100 | tf_op jit(solution)/shard_map/convert_element_type | solution.py:45
  (6 shorter events, 0.1 us)
Async XLA Ops:
  7.0 27.0 %all-to-all-start = ((bf16[128,3,1]{1,2,0:T(2,128)(2,1)}), bf16[128,3,1]{1,2,0:T(2,128)(2,1)S(1)}, u32[]{:S(2)}, u32[]{:S(2)}) async-start(bf16[128,3,1]{1,2,0:T(2,128)(2,1)} %all_to_all.19), calls=%async_computation | async-start | bytes 131072 | tf_op jit(solution)/shard_map/all_to_all | solution.py:30
  34.0 77.4 %all-to-all-start.1 = ((bf16[128,3,5376]{2,1,0:T(4,128)(2,1)}), bf16[128,3,5376]{2,1,0:T(4,128)(2,1)}, u32[]{:S(2)}, u32[]{:S(2)}) async-start(bf16[128,3,5376]{2,1,0:T(4,128)(2,1)} %all_to_all.16), calls=%async_computation.1 | async-start | bytes 11010048 | tf_op jit(solution)/shard_map/all_to_all | solution.py:29
  119.8 70.5 %copy-start = (bf16[256,5376]{1,0:T(8,128)(2,1)S(1)}, bf16[256,5376]{1,0:T(8,128)(2,1)}, u32[]{:S(2)}) copy-start(bf16[256,5376]{1,0:T(8,128)(2,1)} %param.11) | copy-start | bytes 8257540
where the time goes:
time: 202 us; the launch traced here: 201 us
  waiting for transfers between devices  66.8 us (33%)
  blocking collectives  62.9 us (31%)
  local copies, waits for them, and re-layouts  27.9 us (14%)
  starting transfers between devices  21.7 us (11%)
  other arithmetic  13.5 us (7%)
  matrix products  6.88 us (3%)
    all_to_all x1, waiting for transfers between devices, body(): lax.all_to_all(outgoing, ('dp', 'vocab'), split_axis=0, concat_axis=0, ti...  66.8 us
    psum x1, blocking collectives, body(): total = lax.psum(jnp.sum(grad_sum * grad_sum), ('dp', 'vocab'))  62.9 us
    all_to_all x2, local copies, waits for them, and re-layouts, body(): lax.all_to_all(outgoing, ('dp', 'vocab'), split_axis=0, concat_axis=0, ti...  15.9 us
    all_to_all x1, starting transfers between devices, body(): lax.all_to_all(targets, ('dp', 'vocab'), split_axis=0, concat_axis=0, til...  11.5 us
    convert_element_type x1, other arithmetic, body(): return (new_table, first.astype(jnp.bfloat16), second.astype(jnp.bfloat16))  10.8 us
    all_to_all x1, starting transfers between devices, body(): lax.all_to_all(outgoing, ('dp', 'vocab'), split_axis=0, concat_axis=0, ti...  10.2 us
    scatter x1, local copies, waits for them, and re-layouts, body(): jnp.zeros((devices * capacity, width), jnp.bfloat16).at[position]  7.97 us
    dot_general x1, matrix products, body(): grad_sum = jnp.dot(incidence, arrived, preferred_element_type=jnp.float32)  6.88 us
  transfers between devices with their start and end apart: 2, of which 1 were waited for; matrix products, arithmetic and copies ran while one was open for 4% of the time, Pallas kernels for 0%

commit v1 on v0

v1 whole, which is shorter than its diff:
```python
import jax
import jax.numpy as jnp
from jax import lax
from jax.experimental import pallas as pl
from jax.experimental.pallas import tpu as pltpu
from jax.sharding import PartitionSpec as P

AXES = ("dp", "vocab")
SLOTS = 3
CELL = 256
ROWS = 8
BF = jnp.bfloat16
F32 = jnp.float32


def cell_of(piece, slot):
    if piece < 16:
        return piece // 2, 3 * (piece % 2) + slot
    entry = 3 * (piece - 16) + slot
    return entry // 2, 6 + entry % 2


def pattern(piece, column):
    return tuple((cell_of(piece, s)[1], s) for s in range(SLOTS) if cell_of(piece, s)[0] == column)


def iota(shape, dim):
    return lax.broadcasted_iota(jnp.int32, shape, dim)


def pack_kernel(n_dev, holder_ref, offset_ref, grads_ref, out_ref):
    toks = grads_ref.shape[0]
    pieces = grads_ref.shape[1] // CELL
    columns = out_ref.shape[1] // CELL
    holder = holder_ref[...]
    holder_f = holder.astype(F32)
    holder_col = jnp.broadcast_to(holder_f, (128, toks)).T
    halves = []
    for h in range(toks // 128):
        same = (holder_col == holder_f[:, h * 128:(h + 1) * 128]) & (
            iota((toks, 128), 0) < iota((toks, 128), 1) + h * 128)
        halves.append(jnp.sum(same.astype(F32), axis=0, keepdims=True))
    rank_f = jnp.concatenate(halves, axis=1)
    rank = rank_f.astype(jnp.int32)
    rank_col = jnp.broadcast_to(rank_f, (128, toks)).T
    lane = iota((toks, 128), 1).astype(F32)
    rank_hot = jnp.where(rank_col == lane, 1.0, 0.0).astype(BF)
    rank_hot = jnp.concatenate([rank_hot, jnp.zeros_like(rank_hot)], axis=1)
    offset_value = (offset_ref[...] + 1).astype(F32)
    row = iota((n_dev * ROWS, toks), 0)

    def one_hot(pat):
        place = jnp.full((1, toks), -1, jnp.int32)
        for r, s in pat:
            place = jnp.where(rank == s, holder * ROWS + r, place)
        return jnp.where(row == place, 1.0, 0.0).astype(BF)

    made = {}

    def get(pat):
        if pat not in made:
            made[pat] = one_hot(pat)
        return made[pat]

    for k in range(columns):
        left, right = [], []
        for p in range(pieces):
            pat = pattern(p, k)
            if pat:
                left.append(get(pat))
                right.append(grads_ref[:, p * CELL:(p + 1) * CELL])
        if k == columns - 1:
            left.append(jnp.where(row == holder * ROWS + ROWS - 1, offset_value, 0.0).astype(BF))
            right.append(rank_hot)
        out_ref[:, k * CELL:(k + 1) * CELL] = jnp.dot(
            jnp.concatenate(left, axis=1), jnp.concatenate(right, axis=0),
            preferred_element_type=F32).astype(BF)


def sum_kernel(n_dev, arrived_ref, grad_ref, part_ref, wide_ref):
    rows_here = grad_ref.shape[0]
    pieces = grad_ref.shape[1] // CELL
    columns = arrived_ref.shape[1] // CELL
    depth = n_dev * ROWS
    wide_ref[...] = arrived_ref[:, (columns - 1) * CELL:(columns - 1) * CELL + 128].astype(F32)
    tail = wide_ref[pl.ds(ROWS - 1, n_dev, stride=ROWS), :]
    spread = jnp.where(iota((n_dev, depth), 0) == iota((n_dev, depth), 1) // ROWS, 1.0, 0.0).astype(BF)
    target = jnp.dot(tail.T.astype(BF), spread, preferred_element_type=F32).astype(jnp.int32) - 1
    place = iota((1, depth), 1) % ROWS
    row = iota((rows_here, depth), 0)
    made = {}

    def get(pat):
        if pat not in made:
            wanted = jnp.full((1, depth), -1, jnp.int32)
            for r, s in pat:
                wanted = jnp.where(place == r, target[s:s + 1, :], wanted)
            made[pat] = jnp.where(row == wanted, 1.0, 0.0).astype(BF)
        return made[pat]

    total = jnp.zeros((8, CELL), F32)
    for p in range(pieces):
        left, right = [], []
        for k in range(columns):
            pat = pattern(p, k)
            if pat:
                left.append(get(pat))
                right.append(arrived_ref[:, k * CELL:(k + 1) * CELL])
        piece = jnp.dot(jnp.concatenate(left, axis=1), jnp.concatenate(right, axis=0),
                        preferred_element_type=F32)
        grad_ref[:, p * CELL:(p + 1) * CELL] = piece
        total = total + jnp.sum((piece * piece).reshape(rows_here // 8, 8, CELL), axis=0)
    folded = total[:, :128] + total[:, 128:]
    part_ref[...] = jnp.broadcast_to(jnp.sum(folded, axis=0, keepdims=True), part_ref.shape)


def adam_kernel(limit, sums_ref, grad_ref, table_ref, first_ref, second_ref, ot_ref, of_ref, os_ref):
    total = jnp.sum(jnp.sum(sums_ref[...], axis=0, keepdims=True), axis=1, keepdims=True)
    factor = jnp.minimum(1.0, limit / jnp.sqrt(total))
    grad = factor * grad_ref[...]
    first = 0.9 * first_ref[...].astype(F32) + 0.1 * grad
    second = 0.95 * second_ref[...].astype(F32) + 0.05 * grad * grad
    step = first * (0.02 / (1.0 - 0.9**10)) / (jnp.sqrt(second * (1.0 / (1.0 - 0.95**10))) + 1e-8)
    ot_ref[...] = (table_ref[...].astype(F32) - step).astype(BF)
    of_ref[...] = first.astype(BF)
    os_ref[...] = second.astype(BF)


def body(token_grads, row_holder, row_offset, table, first_moment, second_moment):
    n_dev = lax.axis_size("dp") * lax.axis_size("vocab")
    toks, width = token_grads.shape
    rows_here = table.shape[0]
    depth = n_dev * ROWS
    lanes = 8 * CELL
    vmem = pl.BlockSpec(memory_space=pltpu.VMEM)

    with jax.named_scope("pack"):
        outgoing = pl.pallas_call(
            lambda *refs: pack_kernel(n_dev, *refs),
            out_shape=jax.ShapeDtypeStruct((depth, lanes), BF),
            in_specs=[vmem] * 3, out_specs=vmem,
            compiler_params=pltpu.CompilerParams(vmem_limit_bytes=40 * 2**20),
        )(row_holder.reshape(1, toks), row_offset.reshape(1, toks), token_grads)
    with jax.named_scope("exchange"):
        arrived = lax.all_to_all(outgoing, AXES, split_axis=0, concat_axis=0, tiled=True)
    with jax.named_scope("row_sums"):
        grad_sum, part = pl.pallas_call(
            lambda *refs: sum_kernel(n_dev, *refs),
            out_shape=(jax.ShapeDtypeStruct((rows_here, width), F32),
                       jax.ShapeDtypeStruct((n_dev, 128), F32)),
            in_specs=[vmem], out_specs=(vmem, vmem),
            scratch_shapes=[pltpu.VMEM((depth, 128), F32)],
            compiler_params=pltpu.CompilerParams(vmem_limit_bytes=40 * 2**20),
        )(arrived)
    with jax.named_scope("norm"):
        sums = lax.all_to_all(part, AXES, split_axis=0, concat_axis=0, tiled=True)
    limit = 2.0 * float(toks * n_dev * width) ** 0.5
    tall = 32
    block = pl.BlockSpec((tall, width), lambda i: (i, 0))
    with jax.named_scope("adam"):
        return pl.pallas_call(
            lambda *refs: adam_kernel(limit, *refs),
            grid=(rows_here // tall,),
            out_shape=(jax.ShapeDtypeStruct((rows_here, width), BF),) * 3,
            in_specs=[pl.BlockSpec((n_dev, 128), lambda i: (0, 0))] + [block] * 4,
            out_specs=(block,) * 3,
            compiler_params=pltpu.CompilerParams(vmem_limit_bytes=40 * 2**20),
        )(sums, grad_sum, table, first_moment, second_moment)


def solution(mesh):
    rows = P(AXES, None)
    return jax.shard_map(
        body, mesh=mesh,
        in_specs=(rows, rows, P(AXES), rows, rows, rows),
        out_specs=(rows, rows, rows), check_vma=False)
```

time: 202 us -> 101 us (0.50)
  waiting for transfers between devices: 66.8 us -> 0 us
  local copies, waits for them, and re-layouts: 27.9 us -> 3.14 us
  starting transfers between devices: 21.7 us -> 0 us
  Pallas kernels: 0 us -> 17.9 us
  blocking collectives: 62.9 us -> 78.7 us
  other arithmetic: 13.5 us -> 0 us
  matrix products: 6.88 us -> 0 us
    all_to_all x0 -> x2, blocking collectives: none -> 78.7 us  [the longest x1 64.8 us: body(): lax.all_to_all(outgoing, AXES, split_axis=0, concat_axis=0, tiled=True)]
    all_to_all x2 -> x0, waiting for transfers between devices: 66.8 us -> none  [the longest x1 66.8 us: body(): lax.all_to_all(outgoing, ('dp', 'vocab'), split_axis=0, concat_axis=0, ti...]
    psum x1 -> x0, blocking collectives: 62.9 us -> none  [body(): total = lax.psum(jnp.sum(grad_sum * grad_sum), ('dp', 'vocab'))]
    all_to_all x2 -> x0, starting transfers between devices: 21.7 us -> none  [the longest x1 11.5 us: body(): lax.all_to_all(targets, ('dp', 'vocab'), split_axis=0, concat_axis=0, til...]
    pallas_call x0 -> x3, Pallas kernels: none -> 17.9 us  [the longest x1 9.91 us: body(): pl.pallas_call(lambda *refs: adam_kernel(limit, *refs), grid=(rows_here /...]
    all_to_all x3 -> x0, local copies, waits for them, and re-layouts: 16.8 us -> none  [the longest x2 15.9 us: body(): lax.all_to_all(outgoing, ('dp', 'vocab'), split_axis=0, concat_axis=0, ti...]
    convert_element_type x3 -> x0, other arithmetic: 11.7 us -> none  [the longest x1 10.8 us: body(): return (new_table, first.astype(jnp.bfloat16), second.astype(jnp.bfloat16))]
    scatter x2 -> x0, local copies, waits for them, and re-layouts: 10.1 us -> none  [the longest x1 7.97 us: body(): jnp.zeros((devices * capacity, width), jnp.bfloat16).at[position]]
  transfers between devices with their start and end apart: 2 -> 0, of which waited for: 1 -> 0; matrix products, arithmetic and copies ran while one was open for 4% -> 0% of each run, Pallas kernels for 0% -> 0%
where the time goes in v1:
time: 101 us; the launch traced here: 100 us
  blocking collectives  78.7 us (78%)
  Pallas kernels  17.9 us (18%)
  local copies, waits for them, and re-layouts  3.14 us (3%)
    all_to_all x1, blocking collectives, body(): lax.all_to_all(outgoing, AXES, split_axis=0, concat_axis=0, tiled=True)  64.8 us
    all_to_all x1, blocking collectives, body(): sums = lax.all_to_all(part, AXES, split_axis=0, concat_axis=0, tiled=True)  13.9 us
    pallas_call x1, Pallas kernels, body(): pl.pallas_call(lambda *refs: adam_kernel(limit, *refs), grid=(rows_here /...  9.91 us
    pallas_call x1, Pallas kernels, body(): pl.pallas_call(lambda *refs: sum_kernel(n_dev, *refs), out_shape=(jax.Sha...  4.04 us
    pallas_call x1, Pallas kernels, body(): pl.pallas_call(lambda *refs: pack_kernel(n_dev, *refs), out_shape=jax.Sha...  3.95 us
    unnamed x12, local copies, waits for them, and re-layouts  3.14 us

profile of v1, /device:TPU:1, one launch (start us, length us, event | category | flops | bytes accessed | tf_op | source)
XLA Modules:
  0.0 100.4 jit_solution(5136290418187029079)
XLA Ops:
  0.6 0.0 copy-start
  0.6 1.8 %copy-done = bf16[256,5376]{1,0:T(8,128)(2,1)S(1)} copy-done((bf16[256,5376]{1,0:T(8,128)(2,1)S(1)}, bf16[256,5376]{1,0:T(8,128)(2,1)}, u32[]{:S(2)}) %copy-start) | copy-done | bytes 2752536
  2.4 0.0 copy-start.4
  2.4 0.7 copy-done.4
  3.1 0.0 copy-start.5
  3.1 0.7 copy-done.5
  3.8 4.0 %pack.1 = bf16[1024,2048]{1,0:T(8,128)(2,1)S(1)} custom-call(s32[1,256]{1,0:T(1,128)S(1)} %bitcast.12, s32[1,256]{1,0:T(1,128)S(1)} %bitcast.13, bf16[256,5376]{1,0:T(8,128)(2,1)S(1)} %copy-done), custom_call_target="tpu_custom_call" | custom-call | tf_op jit(solution)/shard_map/pack/pallas_call | solution.py:138
  7.7 0.0 copy-start.2
  7.7 0.0 copy-start.3
  7.8 64.8 %all_to_all.22 = bf16[128,8,2048]{2,1,0:T(8,128)(2,1)S(1)} all-to-all(bf16[128,8,2048]{2,1,0:T(8,128)(2,1)S(1)} %bitcast.8), channel_id=1, replica_groups=mesh['dp'=32,'vocab'=4] {'dp','vocab'}, dimensions={0} | all-to-all | bytes 8388608 | tf_op jit(solution)/shard_map/exchange/all_to_all | solution.py:145
  72.5 0.0 copy-start.1
  72.5 4.0 %row_sums.1 = (f32[256,5376]{1,0:T(8,128)S(1)}, f32[128,128]{1,0:T(8,128)S(1)}) custom-call(bf16[1024,2048]{1,0:T(8,128)(2,1)S(1)} %bitcast.9), custom_call_target="tpu_custom_call" | custom-call | tf_op jit(solution)/shard_map/row_sums/pallas_call | solution.py:147
  76.6 13.9 %all_to_all.23 = f32[128,1,128]{2,1,0:T(1,128)S(1)} all-to-all(f32[128,1,128]{2,1,0:T(1,128)S(1)} %bitcast.11), channel_id=1, replica_groups=mesh['dp'=32,'vocab'=4] {'dp','vocab'}, dimensions={0} | all-to-all | bytes 131072 | tf_op jit(solution)/shard_map/norm/all_to_all | solution.py:156
  90.5 0.0 copy-done.2
  90.5 0.0 copy-done.3
  90.5 0.0 copy-done.1
  90.5 9.9 %adam.1 = (bf16[256,5376]{1,0:T(8,128)(2,1)}, bf16[256,5376]{1,0:T(8,128)(2,1)}, bf16[256,5376]{1,0:T(8,128)(2,1)}) custom-call(f32[128,128]{1,0:T(8,128)S(1)} %bitcast.10, f32[256,5376]{1,0:T(8,128)S(1)} %get-tuple-element.6.refs_1_, bf16[256,5376]{1,0:T(8,128)(2,1)S(1)} %copy-done.1, bf16[256,5376]{1,0:T(8,128)(2,1)S(1)} %copy-done.2, ...), custom_call_target="tpu_custom_call" | custom-call | tf_op jit(solution)/shard_map/adam/pallas_call | solution.py:161
Async XLA Ops:
  0.6 1.8 %copy-start = (bf16[256,5376]{1,0:T(8,128)(2,1)S(1)}, bf16[256,5376]{1,0:T(8,128)(2,1)}, u32[]{:S(2)}) copy-start(bf16[256,5376]{1,0:T(8,128)(2,1)} %refs_2_.2) | copy-start | bytes 8257540
  2.4 0.7 copy-start.4
  3.1 0.7 copy-start.5
  7.7 82.7 %copy-start.2 = (bf16[256,5376]{1,0:T(8,128)(2,1)S(1)}, bf16[256,5376]{1,0:T(8,128)(2,1)}, u32[]{:S(2)}) copy-start(bf16[256,5376]{1,0:T(8,128)(2,1)} %refs_3_.1) | copy-start | bytes 8257540
  7.7 82.7 %copy-start.3 = (bf16[256,5376]{1,0:T(8,128)(2,1)S(1)}, bf16[256,5376]{1,0:T(8,128)(2,1)}, u32[]{:S(2)}) copy-start(bf16[256,5376]{1,0:T(8,128)(2,1)} %refs_4_.1) | copy-start | bytes 8257540
  72.5 18.0 %copy-start.1 = (bf16[256,5376]{1,0:T(8,128)(2,1)S(1)}, bf16[256,5376]{1,0:T(8,128)(2,1)}, u32[]{:S(2)}) copy-start(bf16[256,5376]{1,0:T(8,128)(2,1)} %refs_2_.3) | copy-start | bytes 8257540

commit v2 on v1

v2 whole, which is shorter than its diff:
```python
import jax
import jax.numpy as jnp
from jax import lax
from jax.experimental import pallas as pl
from jax.experimental.pallas import tpu as pltpu
from jax.sharding import PartitionSpec as P

AXES = ("dp", "vocab")
SLOTS = 3
CELL = 256
ROWS = 8
TALL = 16
WIDE = 384
BF = jnp.bfloat16
F32 = jnp.float32


def cell_of(piece, slot):
    if piece < 16:
        return piece // 2, 3 * (piece % 2) + slot
    entry = 3 * (piece - 16) + slot
    return entry // 2, 6 + entry % 2


def pattern(piece, column):
    return tuple((cell_of(piece, s)[1], s) for s in range(SLOTS) if cell_of(piece, s)[0] == column)


def iota(shape, dim):
    return lax.broadcasted_iota(jnp.int32, shape, dim)


def pack_kernel(n_dev, holder_hbm, offset_hbm, grads_hbm, out_ref, holder_ref, offset_ref, grads_ref, sems, wide_ref):
    moves = [pltpu.make_async_copy(a, b, sems.at[i]) for i, (a, b) in enumerate(
        ((holder_hbm, holder_ref), (offset_hbm, offset_ref), (grads_hbm, grads_ref)))]
    for move in moves:
        move.start()
    moves[0].wait()
    moves[1].wait()
    toks = grads_ref.shape[0]
    pieces = grads_ref.shape[1] // CELL
    columns = out_ref.shape[1] // CELL
    depth = out_ref.shape[0]
    holder = holder_ref[...]
    holder_f = holder.astype(F32)
    holder_col = jnp.broadcast_to(holder_f, (128, toks)).T
    halves = []
    for h in range(toks // 128):
        same = (holder_col == holder_f[:, h * 128:(h + 1) * 128]) & (
            iota((toks, 128), 0) < iota((toks, 128), 1) + h * 128)
        halves.append(jnp.sum(same.astype(F32), axis=0, keepdims=True))
    rank_f = jnp.concatenate(halves, axis=1)
    rank = rank_f.astype(jnp.int32)
    rank_col = jnp.broadcast_to(rank_f, (128, toks)).T
    lane = iota((toks, 128), 1).astype(F32)
    rank_hot = jnp.where(rank_col == lane, 1.0, 0.0).astype(BF)
    rank_hot = jnp.concatenate([rank_hot, jnp.zeros_like(rank_hot)], axis=1)
    offset_value = (offset_ref[...] + 1).astype(F32)
    row = iota((n_dev, toks), 0)
    hot = jnp.concatenate([
        jnp.where(row == jnp.where(rank == s, holder, -1), 1.0, 0.0).astype(BF) for s in range(SLOTS)], axis=0)
    offset_hot = jnp.where(row == holder, offset_value, 0.0).astype(BF)
    moves[2].wait()

    def put(piece, slot, value):
        column, r = cell_of(piece, slot)
        for c in range(0, CELL, 128):
            wide_ref[pl.ds((column * CELL + c) // 128 * depth + r, n_dev, stride=ROWS), :] = value[:, c:c + 128]

    order = sorted(range(pieces), key=lambda p: (max(cell_of(p, s)[0] for s in range(SLOTS)), p))
    done = 0
    put(pieces, 0, jnp.dot(offset_hot, rank_hot, preferred_element_type=F32))
    for i, p in enumerate(order):
        got = jnp.dot(hot, grads_ref[:, p * CELL:(p + 1) * CELL], preferred_element_type=F32)
        for s in range(SLOTS):
            put(p, s, got[s * n_dev:(s + 1) * n_dev])
        ready = min([cell_of(q, s)[0] for q in order[i + 1:] for s in range(SLOTS)] + [columns])
        if ready > done:
            for t in range(done * CELL // 128, ready * CELL // 128):
                out_ref[:, t * 128:(t + 1) * 128] = wide_ref[t * depth:(t + 1) * depth, :].astype(BF)
            done = ready


def sum_kernel(n_dev, arrived_ref, grad_ref, part_ref, wide_ref):
    rows_here = grad_ref.shape[0]
    pieces = grad_ref.shape[1] // CELL
    columns = arrived_ref.shape[1] // CELL
    depth = arrived_ref.shape[0]

    def take(piece, slot):
        column, r = cell_of(piece, slot)
        return jnp.concatenate([
            wide_ref[pl.ds((column * CELL + c) // 128 * depth + r, n_dev, stride=ROWS), :]
            for c in range(0, CELL, 128)], axis=1)


    def widen(column):
        for t in range(column * CELL // 128, (column + 1) * CELL // 128):
            wide_ref[t * depth:(t + 1) * depth, :] = arrived_ref[:, t * 128:(t + 1) * 128].astype(F32)

    widen(columns - 1)
    target = take(pieces, 0)[:, :128].T.astype(jnp.int32) - 1
    row = iota((rows_here, n_dev), 0)
    hot = jnp.concatenate([
        jnp.where(row == target[s:s + 1, :], 1.0, 0.0).astype(BF) for s in range(SLOTS)], axis=1)
    total = jnp.zeros((8, CELL), F32)
    widened = 0
    order = sorted(range(pieces), key=lambda p: (max(cell_of(p, s)[0] for s in range(SLOTS)), p))
    for p in order:
        need = max(cell_of(p, s)[0] for s in range(SLOTS)) + 1
        for k in range(widened, min(need, columns - 1)):
            widen(k)
        widened = max(widened, need)
        right = jnp.concatenate([take(p, s).astype(BF) for s in range(SLOTS)], axis=0)
        piece = jnp.dot(hot, right, preferred_element_type=F32)
        grad_ref[:, p * CELL:(p + 1) * CELL] = piece
        total = total + jnp.sum((piece * piece).reshape(rows_here // 8, 8, CELL), axis=0)
    folded = total[:, :128] + total[:, 128:]
    part_ref[...] = jnp.broadcast_to(jnp.sum(folded, axis=0, keepdims=True), part_ref.shape)


def adam_kernel(limit, sums_ref, grad_ref, table_ref, first_ref, second_ref, ot_ref, of_ref, os_ref,
                st_ref, sf_ref, ss_ref, sems):
    rows_here, width = grad_ref.shape
    total = jnp.sum(jnp.sum(sums_ref[...], axis=0, keepdims=True), axis=1, keepdims=True)
    factor = jnp.minimum(1.0, limit / jnp.sqrt(total))
    first_gain = 0.1 * factor
    second_gain = 0.05 * (factor * factor)
    root = (1.0 / (1.0 - 0.95**10)) ** 0.5
    scale = 0.02 / (1.0 - 0.9**10) / root
    tiny = 1e-8 / root

    def send(i, what, start):
        return pltpu.make_async_copy(
            (st_ref, sf_ref, ss_ref)[what].at[pl.ds(start, TALL)],
            (ot_ref, of_ref, os_ref)[what].at[pl.ds(start, TALL)], sems.at[what, i])

    def step(i, _):
        start = pl.multiple_of(i * TALL, TALL)
        rows = pl.ds(start, TALL)
        for c in range(0, width, WIDE):
            cols = slice(c, c + WIDE)
            grad = grad_ref[rows, cols]
            first = 0.9 * first_ref[rows, cols].astype(F32) + first_gain * grad
            second = 0.95 * second_ref[rows, cols].astype(F32) + second_gain * (grad * grad)
            bottom = second * lax.rsqrt(second) + tiny
            moved = (scale * first) * pl.reciprocal(bottom, approx=True)
            st_ref[rows, cols] = (table_ref[rows, cols].astype(F32) - moved).astype(BF)
            sf_ref[rows, cols] = first.astype(BF)
            ss_ref[rows, cols] = second.astype(BF)
        for what in range(3):
            send(i, what, start).start()
        return 0

    steps = rows_here // TALL
    lax.fori_loop(0, steps, step, 0)
    for i in range(steps):
        for what in range(3):
            send(i, what, i * TALL).wait()


def body(token_grads, row_holder, row_offset, table, first_moment, second_moment):
    n_dev = lax.axis_size("dp") * lax.axis_size("vocab")
    toks, width = token_grads.shape
    rows_here = table.shape[0]
    depth = n_dev * ROWS
    lanes = 8 * CELL
    vmem = pl.BlockSpec(memory_space=pltpu.VMEM)

    with jax.named_scope("pack"):
        outgoing = pl.pallas_call(
            lambda *refs: pack_kernel(n_dev, *refs),
            out_shape=jax.ShapeDtypeStruct((depth, lanes), BF),
            in_specs=[pl.BlockSpec(memory_space=pltpu.HBM)] * 3, out_specs=vmem,
            scratch_shapes=[pltpu.VMEM((1, toks), jnp.int32), pltpu.VMEM((1, toks), jnp.int32),
                            pltpu.VMEM((toks, width), BF), pltpu.SemaphoreType.DMA((3,)), pltpu.VMEM((lanes // 128 * depth, 128), F32)],
            compiler_params=pltpu.CompilerParams(vmem_limit_bytes=40 * 2**20),
        )(*(pltpu.with_memory_space_constraint(a, pltpu.HBM) for a in (row_holder.reshape(1, toks), row_offset.reshape(1, toks), token_grads)))
    with jax.named_scope("exchange"):
        arrived = lax.all_to_all(outgoing, AXES, split_axis=0, concat_axis=0, tiled=True)
    with jax.named_scope("row_sums"):
        grad_sum, part = pl.pallas_call(
            lambda *refs: sum_kernel(n_dev, *refs),
            out_shape=(jax.ShapeDtypeStruct((rows_here, width), F32),
                       jax.ShapeDtypeStruct((n_dev, 128), F32)),
            in_specs=[vmem], out_specs=(vmem, vmem),
            scratch_shapes=[pltpu.VMEM((lanes // 128 * depth, 128), F32)],
            compiler_params=pltpu.CompilerParams(vmem_limit_bytes=40 * 2**20),
        )(arrived)
    with jax.named_scope("norm"):
        sums = lax.all_to_all(part, AXES, split_axis=0, concat_axis=0, tiled=True)
    limit = 2.0 * float(toks * n_dev * width) ** 0.5
    out = pl.BlockSpec(memory_space=pltpu.HBM)
    with jax.named_scope("adam"):
        return pl.pallas_call(
            lambda *refs: adam_kernel(limit, *refs),
            out_shape=(jax.ShapeDtypeStruct((rows_here, width), BF),) * 3,
            in_specs=[vmem] * 5, out_specs=(out,) * 3,
            scratch_shapes=[pltpu.VMEM((rows_here, width), BF)] * 3
            + [pltpu.SemaphoreType.DMA((3, rows_here // TALL))],
            compiler_params=pltpu.CompilerParams(vmem_limit_bytes=30 * 2**20),
        )(sums, grad_sum, table, first_moment, second_moment)


def solution(mesh):
    rows = P(AXES, None)
    return jax.shard_map(
        body, mesh=mesh,
        in_specs=(rows, rows, P(AXES), rows, rows, rows),
        out_specs=(rows, rows, rows), check_vma=False)
```

time: 101 us -> 91.6 us (0.907)
  Pallas kernels: 17.9 us -> 12.1 us
  local copies, waits for them, and re-layouts: 3.14 us -> 0.02 us
    pallas_call x1, Pallas kernels: 9.91 us -> 5.34 us  [body(): pl.pallas_call(lambda *refs: adam_kernel(limit, *refs), out_shape=(jax.Sh...]
    unnamed x12 -> x6, local copies, waits for them, and re-layouts: 3.14 us -> 0.02 us
    pallas_call x1, Pallas kernels: 4.04 us -> 2.43 us  [body(): pl.pallas_call(lambda *refs: sum_kernel(n_dev, *refs), out_shape=(jax.Sha...]
where the time goes in v2:
time: 91.6 us; the launch traced here: 91.5 us
  blocking collectives  78.7 us (86%)
  Pallas kernels  12.1 us (13%)
    all_to_all x1, blocking collectives, body(): lax.all_to_all(outgoing, AXES, split_axis=0, concat_axis=0, tiled=True)  64.8 us
    all_to_all x1, blocking collectives, body(): sums = lax.all_to_all(part, AXES, split_axis=0, concat_axis=0, tiled=True)  13.9 us
    pallas_call x1, Pallas kernels, body(): pl.pallas_call(lambda *refs: adam_kernel(limit, *refs), out_shape=(jax.Sh...  5.34 us
    pallas_call x1, Pallas kernels, body(): pl.pallas_call(lambda *refs: pack_kernel(n_dev, *refs), out_shape=jax.Sha...  4.38 us
    pallas_call x1, Pallas kernels, body(): pl.pallas_call(lambda *refs: sum_kernel(n_dev, *refs), out_shape=(jax.Sha...  2.43 us

profile of v2, /device:TPU:1, one launch (start us, length us, event | category | flops | bytes accessed | tf_op | source)
XLA Modules:
  0.0 91.5 jit_solution(13254774836276582893)
XLA Ops:
  0.6 4.4 %pack.1 = bf16[1024,2048]{1,0:T(8,128)(2,1)S(1)} custom-call(s32[1,256]{1,0:T(1,128)} %bitcast.12, s32[1,256]{1,0:T(1,128)} %bitcast.13, bf16[256,5376]{1,0:T(8,128)(2,1)} %refs_2_.2), custom_call_target="tpu_custom_call" | custom-call | tf_op jit(solution)/shard_map/pack/pallas_call | solution.py:171
  5.0 0.0 copy-start.1
  5.0 0.0 copy-start.2
  5.0 64.8 %all_to_all.22 = bf16[128,8,2048]{2,1,0:T(8,128)(2,1)S(1)} all-to-all(bf16[128,8,2048]{2,1,0:T(8,128)(2,1)S(1)} %bitcast.8), channel_id=1, replica_groups=mesh['dp'=32,'vocab'=4] {'dp','vocab'}, dimensions={0} | all-to-all | bytes 8388608 | tf_op jit(solution)/shard_map/exchange/all_to_all | solution.py:180
  69.8 0.0 copy-start
  69.8 2.4 %row_sums.1 = (f32[256,5376]{1,0:T(8,128)S(1)}, f32[128,128]{1,0:T(8,128)S(1)}) custom-call(bf16[1024,2048]{1,0:T(8,128)(2,1)S(1)} %bitcast.9), custom_call_target="tpu_custom_call" | custom-call | tf_op jit(solution)/shard_map/row_sums/pallas_call | solution.py:182
  72.2 13.9 %all_to_all.23 = f32[128,1,128]{2,1,0:T(1,128)S(1)} all-to-all(f32[128,1,128]{2,1,0:T(1,128)S(1)} %bitcast.11), channel_id=1, replica_groups=mesh['dp'=32,'vocab'=4] {'dp','vocab'}, dimensions={0} | all-to-all | bytes 131072 | tf_op jit(solution)/shard_map/norm/all_to_all | solution.py:191
  86.1 0.0 copy-done.1
  86.1 0.0 copy-done.2
  86.1 0.0 copy-done
  86.1 5.3 %adam.1 = (bf16[256,5376]{1,0:T(8,128)(2,1)}, bf16[256,5376]{1,0:T(8,128)(2,1)}, bf16[256,5376]{1,0:T(8,128)(2,1)}) custom-call(f32[128,128]{1,0:T(8,128)S(1)} %bitcast.10, f32[256,5376]{1,0:T(8,128)S(1)} %get-tuple-element.6.refs_1_, bf16[256,5376]{1,0:T(8,128)(2,1)S(1)} %copy-done, bf16[256,5376]{1,0:T(8,128)(2,1)S(1)} %copy-done.1, ...), custom_call_target="tpu_custom_call" | custom-call | tf_op jit(solution)/shard_map/adam/pallas_call | solution.py:195
Async XLA Ops:
  5.0 81.1 %copy-start.1 = (bf16[256,5376]{1,0:T(8,128)(2,1)S(1)}, bf16[256,5376]{1,0:T(8,128)(2,1)}, u32[]{:S(2)}) copy-start(bf16[256,5376]{1,0:T(8,128)(2,1)} %refs_3_.1) | copy-start | bytes 8257540
  5.0 81.1 %copy-start.2 = (bf16[256,5376]{1,0:T(8,128)(2,1)S(1)}, bf16[256,5376]{1,0:T(8,128)(2,1)}, u32[]{:S(2)}) copy-start(bf16[256,5376]{1,0:T(8,128)(2,1)} %refs_4_.1) | copy-start | bytes 8257540
  69.8 16.3 %copy-start = (bf16[256,5376]{1,0:T(8,128)(2,1)S(1)}, bf16[256,5376]{1,0:T(8,128)(2,1)}, u32[]{:S(2)}) copy-start(bf16[256,5376]{1,0:T(8,128)(2,1)} %refs_2_.3) | copy-start | bytes 8257540

commit v3 on v2

v3 whole, which is shorter than its diff:
```python
import jax
import jax.numpy as jnp
import numpy as np
from jax import lax
from jax.experimental import pallas as pl
from jax.experimental.pallas import tpu as pltpu
from jax.sharding import PartitionSpec as P

AXES = ("dp", "vocab")
SLOTS = 3
CELL = 256
ROWS = 8
LOADS = (0, 9)
PITCH = 133
TALL = 16
WIDE = 256
BF = jnp.bfloat16
F32 = jnp.float32

OFFSETS = -1


def cell_of(piece, slot):
    if piece < 5:
        entry = 15 if piece == OFFSETS else 3 * piece + slot
        return entry // 2, 6 + entry % 2
    return (piece - 5) // 2, 3 * ((piece - 5) % 2) + slot


def iota(shape, dim):
    return lax.broadcasted_iota(jnp.int32, shape, dim)


def pack_kernel(n_dev, holder_hbm, offset_hbm, grads_hbm, out_ref, holder_ref, offset_ref, grads_ref, sems, *wide_refs):
    toks = grads_ref.shape[0]
    pieces = grads_ref.shape[1] // CELL
    moves = [pltpu.make_async_copy(a, b, sems.at[pieces + i]) for i, (a, b) in enumerate(
        ((holder_hbm, holder_ref), (offset_hbm, offset_ref)))]
    loads = {}
    ends = list(LOADS) + [pieces]
    for p, end in zip(ends, ends[1:]):
        cols = slice(p * CELL, end * CELL)
        loads[p] = pltpu.make_async_copy(grads_hbm.at[:, cols], grads_ref.at[:, cols], sems.at[p])
    for move in moves + list(loads.values())[:1]:
        move.start()
    for move in moves:
        move.wait()
    for load in list(loads.values())[1:]:
        load.start()
    columns = out_ref.shape[1] // CELL
    depth = out_ref.shape[0]
    holder = holder_ref[...]
    holder_f = holder.astype(F32)
    holder_col = jnp.broadcast_to(holder_f, (128, toks)).T
    halves = []
    for h in range(toks // 128):
        same = (holder_col == holder_f[:, h * 128:(h + 1) * 128]) & (
            iota((toks, 128), 0) < iota((toks, 128), 1) + h * 128)
        halves.append(jnp.sum(same.astype(F32), axis=0, keepdims=True))
    rank_f = jnp.concatenate(halves, axis=1)
    rank = rank_f.astype(jnp.int32)
    rank_col = jnp.broadcast_to(rank_f, (128, toks)).T
    lane = iota((toks, 128), 1).astype(F32)
    rank_hot = jnp.where(rank_col == lane, 1.0, 0.0).astype(BF)
    rank_hot = jnp.concatenate([rank_hot, jnp.zeros_like(rank_hot)], axis=1)
    offset_value = (offset_ref[...] + 1).astype(F32)
    row = iota((n_dev, toks), 0)
    hot = jnp.concatenate([
        jnp.where(row == jnp.where(rank == s, holder, -1), 1.0, 0.0).astype(BF) for s in range(SLOTS)], axis=0)
    offset_hot = jnp.where(row == holder, offset_value, 0.0).astype(BF)

    def put(piece, slot, value):
        column, r = cell_of(piece, slot)
        for c in range(0, CELL, 128):
            wide_refs[column][pl.ds(c // 128 * depth + r, n_dev, stride=ROWS), :] = value[:, c:c + 128]

    done = 0
    put(OFFSETS, 0, jnp.dot(offset_hot, rank_hot, preferred_element_type=F32))
    for p in range(pieces):
        if p in loads:
            loads[p].wait()
        got = jnp.dot(hot, grads_ref[:, p * CELL:(p + 1) * CELL], preferred_element_type=F32)
        for s in range(SLOTS):
            put(p, s, got[s * n_dev:(s + 1) * n_dev])
        ready = min([cell_of(q, s)[0] for q in range(p + 1, pieces) for s in range(SLOTS)] + [columns])
        for column in range(done, ready):
            for row0 in range(0, depth, 64):
                out_ref[row0:row0 + 64, column * CELL:(column + 1) * CELL] = jnp.concatenate(
                    [wide_refs[column][t * depth + row0:t * depth + row0 + 64, :] for t in range(CELL // 128)],
                    axis=1).astype(BF)
        done = max(done, ready)


def sum_kernel(n_dev, arrived_ref, grad_ref, part_ref, *wide_refs):
    rows_here = grad_ref.shape[0]
    pieces = grad_ref.shape[1] // CELL
    columns = arrived_ref.shape[1] // CELL
    depth = arrived_ref.shape[0]

    def take(piece, slot):
        column, r = cell_of(piece, slot)
        return jnp.concatenate([
            wide_refs[column][(c // 128 * ROWS + r) * PITCH:(c // 128 * ROWS + r) * PITCH + n_dev, :]
            for c in range(0, CELL, 128)], axis=1)

    def widen(column):
        both = arrived_ref[:, column * CELL:(column + 1) * CELL].astype(F32)
        for t in range(CELL // 128):
            for source in range(n_dev):
                wide_refs[column][pl.ds(t * ROWS * PITCH + source, ROWS, stride=PITCH), :] = both[
                    source * ROWS:(source + 1) * ROWS, t * 128:(t + 1) * 128]

    widen(columns - 1)
    target = take(OFFSETS, 0)[:, :128].T.astype(jnp.int32) - 1
    row = iota((rows_here, n_dev), 0)
    hot = jnp.concatenate([
        jnp.where(row == target[s:s + 1, :], 1.0, 0.0).astype(BF) for s in range(SLOTS)], axis=1)
    total = jnp.zeros((8, CELL), F32)
    widened = 0
    for p in list(range(5, pieces)) + list(range(5)):
        need = max(cell_of(p, s)[0] for s in range(SLOTS)) + 1
        for k in range(widened, min(need, columns - 1)):
            widen(k)
        widened = max(widened, need)
        right = jnp.concatenate([take(p, s).astype(BF) for s in range(SLOTS)], axis=0)
        piece = jnp.dot(hot, right, preferred_element_type=F32)
        grad_ref[:, p * CELL:(p + 1) * CELL] = piece
        total = total + jnp.sum((piece * piece).reshape(rows_here // 8, 8, CELL), axis=0)
    folded = total[:, :128] + total[:, 128:]
    part_ref[...] = jnp.broadcast_to(jnp.sum(folded, axis=0, keepdims=True), part_ref.shape)


def adam_kernel(limit, sums_ref, grad_ref, first_ref, second_ref, table_ref, ot_ref, of_ref, os_ref,
                st_ref, sf_ref, ss_ref, sems):
    rows_here, width = grad_ref.shape
    total = jnp.sum(jnp.sum(sums_ref[...], axis=0, keepdims=True), axis=1, keepdims=True)
    factor = jnp.minimum(1.0, limit / jnp.sqrt(total))
    first_gain = 0.1 * factor
    second_gain = 0.05 * (factor * factor)
    root = (1.0 / (1.0 - 0.95**10)) ** 0.5
    scale = 0.02 / (1.0 - 0.9**10) / root
    tiny = 1e-8 / root

    def scaled(matrix, values):
        return jnp.dot(matrix, jnp.concatenate([values] * 3, axis=0), preferred_element_type=F32)

    def times(value):
        parts, value = [], float(np.float32(value))
        for _ in range(3):
            parts.insert(0, float(np.float32(value).astype(BF)))
            value -= parts[0]
        row, column = iota((TALL, 3 * TALL), 0), iota((TALL, 3 * TALL), 1)
        which = jnp.where(column < TALL, parts[0], jnp.where(column < 2 * TALL, parts[1], parts[2]))
        return jnp.where(row == column % TALL, which, 0.0).astype(BF)

    first_mat, second_mat = times(0.9), times(0.95)

    def send(i, what):
        rows = pl.ds(i * TALL, TALL)
        return pltpu.make_async_copy(
            (st_ref, sf_ref, ss_ref)[what].at[rows], (ot_ref, of_ref, os_ref)[what].at[rows], sems.at[what, i])

    for i in range(rows_here // TALL):
        rows = slice(i * TALL, (i + 1) * TALL)
        for c in range(0, width, WIDE):
            cols = slice(c, c + WIDE)
            grad = grad_ref[rows, cols]
            first = scaled(first_mat, first_ref[rows, cols]) + first_gain * grad
            second = scaled(second_mat, second_ref[rows, cols]) + second_gain * (grad * grad)
            bottom = second * lax.rsqrt(second) + tiny
            moved = (scale * first) * pl.reciprocal(bottom, approx=True)
            st_ref[rows, cols] = (table_ref[rows, cols].astype(F32) - moved).astype(BF)
            sf_ref[rows, cols] = first.astype(BF)
            ss_ref[rows, cols] = second.astype(BF)
        for what in range(3):
            send(i, what).start()
    for i in range(rows_here // TALL):
        for what in range(3):
            send(i, what).wait()


def body(token_grads, row_holder, row_offset, table, first_moment, second_moment):
    n_dev = lax.axis_size("dp") * lax.axis_size("vocab")
    toks, width = token_grads.shape
    rows_here = table.shape[0]
    depth = n_dev * ROWS
    lanes = 8 * CELL
    vmem = pl.BlockSpec(memory_space=pltpu.VMEM)

    with jax.named_scope("pack"):
        outgoing = pl.pallas_call(
            lambda *refs: pack_kernel(n_dev, *refs),
            out_shape=jax.ShapeDtypeStruct((depth, lanes), BF),
            in_specs=[pl.BlockSpec(memory_space=pltpu.HBM)] * 3, out_specs=vmem,
            scratch_shapes=[pltpu.VMEM((1, toks), jnp.int32), pltpu.VMEM((1, toks), jnp.int32),
                            pltpu.VMEM((toks, width), BF), pltpu.SemaphoreType.DMA((width // CELL + 2,))]
            + [pltpu.VMEM((CELL // 128 * depth, 128), F32)] * (lanes // CELL),
            compiler_params=pltpu.CompilerParams(vmem_limit_bytes=40 * 2**20),
        )(*(pltpu.with_memory_space_constraint(a, pltpu.HBM) for a in (
            row_holder.reshape(1, toks), row_offset.reshape(1, toks), token_grads)))
    with jax.named_scope("exchange"):
        arrived = lax.all_to_all(outgoing, AXES, split_axis=0, concat_axis=0, tiled=True)
    with jax.named_scope("row_sums"):
        grad_sum, part = pl.pallas_call(
            lambda *refs: sum_kernel(n_dev, *refs),
            out_shape=(jax.ShapeDtypeStruct((rows_here, width), F32),
                       jax.ShapeDtypeStruct((n_dev, 128), F32)),
            in_specs=[vmem], out_specs=(vmem, vmem),
            scratch_shapes=[pltpu.VMEM((CELL // 128 * ROWS * PITCH, 128), F32)] * (lanes // CELL),
            compiler_params=pltpu.CompilerParams(vmem_limit_bytes=40 * 2**20),
        )(arrived)
    with jax.named_scope("norm"):
        sums = lax.all_to_all(part, AXES, split_axis=0, concat_axis=0, tiled=True)
    limit = 2.0 * float(toks * n_dev * width) ** 0.5
    out = pl.BlockSpec(memory_space=pltpu.HBM)
    with jax.named_scope("adam"):
        return pl.pallas_call(
            lambda *refs: adam_kernel(limit, *refs),
            out_shape=(jax.ShapeDtypeStruct((rows_here, width), BF),) * 3,
            in_specs=[vmem] * 5, out_specs=(out,) * 3,
            scratch_shapes=[pltpu.VMEM((rows_here, width), BF)] * 3
            + [pltpu.SemaphoreType.DMA((3, rows_here // TALL))],
            compiler_params=pltpu.CompilerParams(vmem_limit_bytes=30 * 2**20),
        )(sums, grad_sum, first_moment, second_moment, table)


def solution(mesh):
    rows = P(AXES, None)
    return jax.shard_map(
        body, mesh=mesh,
        in_specs=(rows, rows, P(AXES), rows, rows, rows),
        out_specs=(rows, rows, rows), check_vma=False)
```

time: 91.6 us -> 90.1 us (0.984)
  Pallas kernels: 12.1 us -> 10.6 us
    pallas_call x1, Pallas kernels: 5.34 us -> 4.35 us  [body(): pl.pallas_call(lambda *refs: adam_kernel(limit, *refs), out_shape=(jax.Sh...]
where the time goes in v3:
time: 90.1 us; the launch traced here: 89.9 us
  blocking collectives  78.7 us (87%)
  Pallas kernels  10.6 us (12%)
    all_to_all x1, blocking collectives, body(): lax.all_to_all(outgoing, AXES, split_axis=0, concat_axis=0, tiled=True)  64.8 us
    all_to_all x1, blocking collectives, body(): sums = lax.all_to_all(part, AXES, split_axis=0, concat_axis=0, tiled=True)  13.9 us
    pallas_call x1, Pallas kernels, body(): pl.pallas_call(lambda *refs: adam_kernel(limit, *refs), out_shape=(jax.Sh...  4.35 us
    pallas_call x1, Pallas kernels, body(): pl.pallas_call(lambda *refs: pack_kernel(n_dev, *refs), out_shape=jax.Sha...  4.14 us
    pallas_call x1, Pallas kernels, body(): pl.pallas_call(lambda *refs: sum_kernel(n_dev, *refs), out_shape=(jax.Sha...  2.09 us

profile of v3, /device:TPU:1, one launch (start us, length us, event | category | flops | bytes accessed | tf_op | source)
XLA Modules:
  0.0 89.9 jit_solution(17884002405357408420)
XLA Ops:
  0.6 4.1 %pack.1 = bf16[1024,2048]{1,0:T(8,128)(2,1)S(1)} custom-call(s32[1,256]{1,0:T(1,128)} %bitcast.12, s32[1,256]{1,0:T(1,128)} %bitcast.13, bf16[256,5376]{1,0:T(8,128)(2,1)} %refs_2_.2), custom_call_target="tpu_custom_call" | custom-call | tf_op jit(solution)/shard_map/pack/pallas_call | solution.py:191
  4.8 0.0 copy-start.1
  4.8 0.0 copy-start.2
  4.8 64.8 %all_to_all.22 = bf16[128,8,2048]{2,1,0:T(8,128)(2,1)S(1)} all-to-all(bf16[128,8,2048]{2,1,0:T(8,128)(2,1)S(1)} %bitcast.8), channel_id=1, replica_groups=mesh['dp'=32,'vocab'=4] {'dp','vocab'}, dimensions={0} | all-to-all | bytes 8388608 | tf_op jit(solution)/shard_map/exchange/all_to_all | solution.py:202
  69.6 0.0 copy-start
  69.6 2.1 %row_sums.1 = (f32[256,5376]{1,0:T(8,128)S(1)}, f32[128,128]{1,0:T(8,128)S(1)}) custom-call(bf16[1024,2048]{1,0:T(8,128)(2,1)S(1)} %bitcast.9), custom_call_target="tpu_custom_call" | custom-call | tf_op jit(solution)/shard_map/row_sums/pallas_call | solution.py:204
  71.7 13.9 %all_to_all.23 = f32[128,1,128]{2,1,0:T(1,128)S(1)} all-to-all(f32[128,1,128]{2,1,0:T(1,128)S(1)} %bitcast.11), channel_id=1, replica_groups=mesh['dp'=32,'vocab'=4] {'dp','vocab'}, dimensions={0} | all-to-all | bytes 131072 | tf_op jit(solution)/shard_map/norm/all_to_all | solution.py:213
  85.6 0.0 copy-done.1
  85.6 0.0 copy-done.2
  85.6 0.0 copy-done
  85.6 4.4 %adam.1 = (bf16[256,5376]{1,0:T(8,128)(2,1)}, bf16[256,5376]{1,0:T(8,128)(2,1)}, bf16[256,5376]{1,0:T(8,128)(2,1)}) custom-call(f32[128,128]{1,0:T(8,128)S(1)} %bitcast.10, f32[256,5376]{1,0:T(8,128)S(1)} %get-tuple-element.6.refs_1_, bf16[256,5376]{1,0:T(8,128)(2,1)S(1)} %copy-done, bf16[256,5376]{1,0:T(8,128)(2,1)S(1)} %copy-done.1, ...), custom_call_target="tpu_custom_call" | custom-call | tf_op jit(solution)/shard_map/adam/pallas_call | solution.py:217
Async XLA Ops:
  4.8 80.8 %copy-start.1 = (bf16[256,5376]{1,0:T(8,128)(2,1)S(1)}, bf16[256,5376]{1,0:T(8,128)(2,1)}, u32[]{:S(2)}) copy-start(bf16[256,5376]{1,0:T(8,128)(2,1)} %refs_3_.1) | copy-start | bytes 8257540
  4.8 80.8 %copy-start.2 = (bf16[256,5376]{1,0:T(8,128)(2,1)S(1)}, bf16[256,5376]{1,0:T(8,128)(2,1)}, u32[]{:S(2)}) copy-start(bf16[256,5376]{1,0:T(8,128)(2,1)} %refs_4_.1) | copy-start | bytes 8257540
  69.6 16.0 %copy-start = (bf16[256,5376]{1,0:T(8,128)(2,1)S(1)}, bf16[256,5376]{1,0:T(8,128)(2,1)}, u32[]{:S(2)}) copy-start(bf16[256,5376]{1,0:T(8,128)(2,1)} %refs_2_.3) | copy-start | bytes 8257540

commit v4 on v3

--- a/solution.py
+++ b/solution.py
@@ -127,14 +127,14 @@
         grad_ref[:, p * CELL:(p + 1) * CELL] = piece
         total = total + jnp.sum((piece * piece).reshape(rows_here // 8, 8, CELL), axis=0)
     folded = total[:, :128] + total[:, 128:]
-    part_ref[...] = jnp.broadcast_to(jnp.sum(folded, axis=0, keepdims=True), part_ref.shape)
+    part_ref[...] = jnp.broadcast_to(jnp.sum(jnp.sum(folded, axis=0, keepdims=True), axis=1, keepdims=True), part_ref.shape)
 
 
 def adam_kernel(limit, sums_ref, grad_ref, first_ref, second_ref, table_ref, ot_ref, of_ref, os_ref,
                 st_ref, sf_ref, ss_ref, sems):
     rows_here, width = grad_ref.shape
-    total = jnp.sum(jnp.sum(sums_ref[...], axis=0, keepdims=True), axis=1, keepdims=True)
-    factor = jnp.minimum(1.0, limit / jnp.sqrt(total))
+    total = jnp.sum(sums_ref[...], axis=0, keepdims=True)[:, :1]
+    factor = jnp.minimum(1.0, limit * lax.rsqrt(total))
     first_gain = 0.1 * factor
     second_gain = 0.05 * (factor * factor)
     root = (1.0 / (1.0 - 0.95**10)) ** 0.5

time: 90.1 us -> 89.8 us (level)
  no operation moved by 1% of the time
where the time goes in v4:
time: 89.8 us; the launch traced here: 89.6 us
  blocking collectives  78.7 us (88%)
  Pallas kernels  10.3 us (11%)
    all_to_all x1, blocking collectives, body(): lax.all_to_all(outgoing, AXES, split_axis=0, concat_axis=0, tiled=True)  64.8 us
    all_to_all x1, blocking collectives, body(): sums = lax.all_to_all(part, AXES, split_axis=0, concat_axis=0, tiled=True)  13.9 us
    pallas_call x1, Pallas kernels, body(): pl.pallas_call(lambda *refs: pack_kernel(n_dev, *refs), out_shape=jax.Sha...  4.14 us
    pallas_call x1, Pallas kernels, body(): pl.pallas_call(lambda *refs: adam_kernel(limit, *refs), out_shape=(jax.Sh...  3.99 us
    pallas_call x1, Pallas kernels, body(): pl.pallas_call(lambda *refs: sum_kernel(n_dev, *refs), out_shape=(jax.Sha...  2.16 us

profile of v4, /device:TPU:1, one launch (start us, length us, event | category | flops | bytes accessed | tf_op | source)
XLA Modules:
  0.0 89.6 jit_solution(7181692452264749222)
XLA Ops:
  0.6 4.1 %pack.1 = bf16[1024,2048]{1,0:T(8,128)(2,1)S(1)} custom-call(s32[1,256]{1,0:T(1,128)} %bitcast.12, s32[1,256]{1,0:T(1,128)} %bitcast.13, bf16[256,5376]{1,0:T(8,128)(2,1)} %refs_2_.2), custom_call_target="tpu_custom_call" | custom-call | tf_op jit(solution)/shard_map/pack/pallas_call | solution.py:191
  4.8 0.0 copy-start.1
  4.8 0.0 copy-start.2
  4.8 64.8 %all_to_all.22 = bf16[128,8,2048]{2,1,0:T(8,128)(2,1)S(1)} all-to-all(bf16[128,8,2048]{2,1,0:T(8,128)(2,1)S(1)} %bitcast.8), channel_id=1, replica_groups=mesh['dp'=32,'vocab'=4] {'dp','vocab'}, dimensions={0} | all-to-all | bytes 8388608 | tf_op jit(solution)/shard_map/exchange/all_to_all | solution.py:202
  69.6 0.0 copy-start
  69.6 2.2 %row_sums.1 = (f32[256,5376]{1,0:T(8,128)S(1)}, f32[128,128]{1,0:T(8,128)S(1)}) custom-call(bf16[1024,2048]{1,0:T(8,128)(2,1)S(1)} %bitcast.9), custom_call_target="tpu_custom_call" | custom-call | tf_op jit(solution)/shard_map/row_sums/pallas_call | solution.py:204
  71.7 13.9 %all_to_all.23 = f32[128,1,128]{2,1,0:T(1,128)S(1)} all-to-all(f32[128,1,128]{2,1,0:T(1,128)S(1)} %bitcast.11), channel_id=1, replica_groups=mesh['dp'=32,'vocab'=4] {'dp','vocab'}, dimensions={0} | all-to-all | bytes 131072 | tf_op jit(solution)/shard_map/norm/all_to_all | solution.py:213
  85.6 0.0 copy-done.1
  85.6 0.0 copy-done.2
  85.6 0.0 copy-done
  85.6 4.0 %adam.1 = (bf16[256,5376]{1,0:T(8,128)(2,1)}, bf16[256,5376]{1,0:T(8,128)(2,1)}, bf16[256,5376]{1,0:T(8,128)(2,1)}) custom-call(f32[128,128]{1,0:T(8,128)S(1)} %bitcast.10, f32[256,5376]{1,0:T(8,128)S(1)} %get-tuple-element.6.refs_1_, bf16[256,5376]{1,0:T(8,128)(2,1)S(1)} %copy-done, bf16[256,5376]{1,0:T(8,128)(2,1)S(1)} %copy-done.1, ...), custom_call_target="tpu_custom_call" | custom-call | tf_op jit(solution)/shard_map/adam/pallas_call | solution.py:217
Async XLA Ops:
  4.8 80.8 %copy-start.1 = (bf16[256,5376]{1,0:T(8,128)(2,1)S(1)}, bf16[256,5376]{1,0:T(8,128)(2,1)}, u32[]{:S(2)}) copy-start(bf16[256,5376]{1,0:T(8,128)(2,1)} %refs_3_.1) | copy-start | bytes 8257540
  4.8 80.8 %copy-start.2 = (bf16[256,5376]{1,0:T(8,128)(2,1)S(1)}, bf16[256,5376]{1,0:T(8,128)(2,1)}, u32[]{:S(2)}) copy-start(bf16[256,5376]{1,0:T(8,128)(2,1)} %refs_4_.1) | copy-start | bytes 8257540
  69.6 16.1 %copy-start = (bf16[256,5376]{1,0:T(8,128)(2,1)S(1)}, bf16[256,5376]{1,0:T(8,128)(2,1)}, u32[]{:S(2)}) copy-start(bf16[256,5376]{1,0:T(8,128)(2,1)} %refs_2_.3) | copy-start | bytes 8257540

commit v5 on v4

--- a/solution.py
+++ b/solution.py
@@ -11,6 +11,7 @@
 CELL = 256
 ROWS = 8
 LOADS = (0, 9)
+SPACING = 9
 PITCH = 133
 TALL = 16
 WIDE = 256
@@ -72,7 +73,7 @@
     def put(piece, slot, value):
         column, r = cell_of(piece, slot)
         for c in range(0, CELL, 128):
-            wide_refs[column][pl.ds(c // 128 * depth + r, n_dev, stride=ROWS), :] = value[:, c:c + 128]
+            wide_refs[column][pl.ds(c // 128 * n_dev * SPACING + r, n_dev, stride=SPACING), :] = value[:, c:c + 128]
 
     done = 0
     put(OFFSETS, 0, jnp.dot(offset_hot, rank_hot, preferred_element_type=F32))
@@ -84,10 +85,11 @@
             put(p, s, got[s * n_dev:(s + 1) * n_dev])
         ready = min([cell_of(q, s)[0] for q in range(p + 1, pieces) for s in range(SLOTS)] + [columns])
         for column in range(done, ready):
-            for row0 in range(0, depth, 64):
-                out_ref[row0:row0 + 64, column * CELL:(column + 1) * CELL] = jnp.concatenate(
-                    [wide_refs[column][t * depth + row0:t * depth + row0 + 64, :] for t in range(CELL // 128)],
-                    axis=1).astype(BF)
+            for d in range(0, n_dev, 8):
+                out_ref[d * ROWS:(d + 8) * ROWS, column * CELL:(column + 1) * CELL] = jnp.concatenate([
+                    jnp.concatenate([wide_refs[column][(t * n_dev + e) * SPACING:(t * n_dev + e) * SPACING + ROWS, :]
+                                     for e in range(d, d + 8)], axis=0)
+                    for t in range(CELL // 128)], axis=1).astype(BF)
         done = max(done, ready)
 
 
@@ -194,7 +196,7 @@
             in_specs=[pl.BlockSpec(memory_space=pltpu.HBM)] * 3, out_specs=vmem,
             scratch_shapes=[pltpu.VMEM((1, toks), jnp.int32), pltpu.VMEM((1, toks), jnp.int32),
                             pltpu.VMEM((toks, width), BF), pltpu.SemaphoreType.DMA((width // CELL + 2,))]
-            + [pltpu.VMEM((CELL // 128 * depth, 128), F32)] * (lanes // CELL),
+            + [pltpu.VMEM((CELL // 128 * n_dev * SPACING, 128), F32)] * (lanes // CELL),
             compiler_params=pltpu.CompilerParams(vmem_limit_bytes=40 * 2**20),
         )(*(pltpu.with_memory_space_constraint(a, pltpu.HBM) for a in (
             row_holder.reshape(1, toks), row_offset.reshape(1, toks), token_grads)))

time: 89.8 us -> 89.2 us (level)
  no operation moved by 1% of the time
where the time goes in v5:
time: 89.2 us; the launch traced here: 89 us
  blocking collectives  78.7 us (88%)
  Pallas kernels  9.66 us (11%)
    all_to_all x1, blocking collectives, body(): lax.all_to_all(outgoing, AXES, split_axis=0, concat_axis=0, tiled=True)  64.8 us
    all_to_all x1, blocking collectives, body(): sums = lax.all_to_all(part, AXES, split_axis=0, concat_axis=0, tiled=True)  13.9 us
    pallas_call x1, Pallas kernels, body(): pl.pallas_call(lambda *refs: adam_kernel(limit, *refs), out_shape=(jax.Sh...  3.99 us
    pallas_call x1, Pallas kernels, body(): pl.pallas_call(lambda *refs: pack_kernel(n_dev, *refs), out_shape=jax.Sha...  3.51 us
    pallas_call x1, Pallas kernels, body(): pl.pallas_call(lambda *refs: sum_kernel(n_dev, *refs), out_shape=(jax.Sha...  2.16 us

profile of v5, /device:TPU:1, one launch (start us, length us, event | category | flops | bytes accessed | tf_op | source)
XLA Modules:
  0.0 89.0 jit_solution(2040645820925676916)
XLA Ops:
  0.6 3.5 %pack.1 = bf16[1024,2048]{1,0:T(8,128)(2,1)S(1)} custom-call(s32[1,256]{1,0:T(1,128)} %bitcast.12, s32[1,256]{1,0:T(1,128)} %bitcast.13, bf16[256,5376]{1,0:T(8,128)(2,1)} %refs_2_.2), custom_call_target="tpu_custom_call" | custom-call | tf_op jit(solution)/shard_map/pack/pallas_call | solution.py:193
  4.1 0.0 copy-start.1
  4.2 0.0 copy-start.2
  4.2 64.8 %all_to_all.22 = bf16[128,8,2048]{2,1,0:T(8,128)(2,1)S(1)} all-to-all(bf16[128,8,2048]{2,1,0:T(8,128)(2,1)S(1)} %bitcast.8), channel_id=1, replica_groups=mesh['dp'=32,'vocab'=4] {'dp','vocab'}, dimensions={0} | all-to-all | bytes 8388608 | tf_op jit(solution)/shard_map/exchange/all_to_all | solution.py:204
  68.9 0.0 copy-start
  68.9 2.2 %row_sums.1 = (f32[256,5376]{1,0:T(8,128)S(1)}, f32[128,128]{1,0:T(8,128)S(1)}) custom-call(bf16[1024,2048]{1,0:T(8,128)(2,1)S(1)} %bitcast.9), custom_call_target="tpu_custom_call" | custom-call | tf_op jit(solution)/shard_map/row_sums/pallas_call | solution.py:206
  71.1 13.9 %all_to_all.23 = f32[128,1,128]{2,1,0:T(1,128)S(1)} all-to-all(f32[128,1,128]{2,1,0:T(1,128)S(1)} %bitcast.11), channel_id=1, replica_groups=mesh['dp'=32,'vocab'=4] {'dp','vocab'}, dimensions={0} | all-to-all | bytes 131072 | tf_op jit(solution)/shard_map/norm/all_to_all | solution.py:215
  85.0 0.0 copy-done.1
  85.0 0.0 copy-done.2
  85.0 0.0 copy-done
  85.0 4.0 %adam.1 = (bf16[256,5376]{1,0:T(8,128)(2,1)}, bf16[256,5376]{1,0:T(8,128)(2,1)}, bf16[256,5376]{1,0:T(8,128)(2,1)}) custom-call(f32[128,128]{1,0:T(8,128)S(1)} %bitcast.10, f32[256,5376]{1,0:T(8,128)S(1)} %get-tuple-element.6.refs_1_, bf16[256,5376]{1,0:T(8,128)(2,1)S(1)} %copy-done, bf16[256,5376]{1,0:T(8,128)(2,1)S(1)} %copy-done.1, ...), custom_call_target="tpu_custom_call" | custom-call | tf_op jit(solution)/shard_map/adam/pallas_call | solution.py:219
Async XLA Ops:
  4.1 80.8 %copy-start.1 = (bf16[256,5376]{1,0:T(8,128)(2,1)S(1)}, bf16[256,5376]{1,0:T(8,128)(2,1)}, u32[]{:S(2)}) copy-start(bf16[256,5376]{1,0:T(8,128)(2,1)} %refs_3_.1) | copy-start | bytes 8257540
  4.2 80.8 %copy-start.2 = (bf16[256,5376]{1,0:T(8,128)(2,1)S(1)}, bf16[256,5376]{1,0:T(8,128)(2,1)}, u32[]{:S(2)}) copy-start(bf16[256,5376]{1,0:T(8,128)(2,1)} %refs_4_.1) | copy-start | bytes 8257540
  68.9 16.1 %copy-start = (bf16[256,5376]{1,0:T(8,128)(2,1)S(1)}, bf16[256,5376]{1,0:T(8,128)(2,1)}, u32[]{:S(2)}) copy-start(bf16[256,5376]{1,0:T(8,128)(2,1)} %refs_2_.3) | copy-start | bytes 8257540

commit v6 on v5

--- a/solution.py
+++ b/solution.py
@@ -10,7 +10,7 @@
 SLOTS = 3
 CELL = 256
 ROWS = 8
-LOADS = (0, 9)
+LOADS = (0, 11)
 SPACING = 9
 PITCH = 133
 TALL = 16

time: 89.2 us -> 89.1 us (level)
  no operation moved by 1% of the time
where the time goes in v6:
time: 89.1 us; the launch traced here: 89 us
  blocking collectives  78.7 us (88%)
  Pallas kernels  9.62 us (11%)
    all_to_all x1, blocking collectives, body(): lax.all_to_all(outgoing, AXES, split_axis=0, concat_axis=0, tiled=True)  64.8 us
    all_to_all x1, blocking collectives, body(): sums = lax.all_to_all(part, AXES, split_axis=0, concat_axis=0, tiled=True)  13.9 us
    pallas_call x1, Pallas kernels, body(): pl.pallas_call(lambda *refs: adam_kernel(limit, *refs), out_shape=(jax.Sh...  3.99 us
    pallas_call x1, Pallas kernels, body(): pl.pallas_call(lambda *refs: pack_kernel(n_dev, *refs), out_shape=jax.Sha...  3.47 us
    pallas_call x1, Pallas kernels, body(): pl.pallas_call(lambda *refs: sum_kernel(n_dev, *refs), out_shape=(jax.Sha...  2.16 us

profile of v6, /device:TPU:1, one launch (start us, length us, event | category | flops | bytes accessed | tf_op | source)
XLA Modules:
  0.0 89.0 jit_solution(12919769374108731689)
XLA Ops:
  0.6 3.5 %pack.1 = bf16[1024,2048]{1,0:T(8,128)(2,1)S(1)} custom-call(s32[1,256]{1,0:T(1,128)} %bitcast.12, s32[1,256]{1,0:T(1,128)} %bitcast.13, bf16[256,5376]{1,0:T(8,128)(2,1)} %refs_2_.2), custom_call_target="tpu_custom_call" | custom-call | tf_op jit(solution)/shard_map/pack/pallas_call | solution.py:193
  4.1 0.0 copy-start.1
  4.1 0.0 copy-start.2
  4.1 64.8 %all_to_all.22 = bf16[128,8,2048]{2,1,0:T(8,128)(2,1)S(1)} all-to-all(bf16[128,8,2048]{2,1,0:T(8,128)(2,1)S(1)} %bitcast.8), channel_id=1, replica_groups=mesh['dp'=32,'vocab'=4] {'dp','vocab'}, dimensions={0} | all-to-all | bytes 8388608 | tf_op jit(solution)/shard_map/exchange/all_to_all | solution.py:204
  68.9 0.0 copy-start
  68.9 2.2 %row_sums.1 = (f32[256,5376]{1,0:T(8,128)S(1)}, f32[128,128]{1,0:T(8,128)S(1)}) custom-call(bf16[1024,2048]{1,0:T(8,128)(2,1)S(1)} %bitcast.9), custom_call_target="tpu_custom_call" | custom-call | tf_op jit(solution)/shard_map/row_sums/pallas_call | solution.py:206
  71.1 13.9 %all_to_all.23 = f32[128,1,128]{2,1,0:T(1,128)S(1)} all-to-all(f32[128,1,128]{2,1,0:T(1,128)S(1)} %bitcast.11), channel_id=1, replica_groups=mesh['dp'=32,'vocab'=4] {'dp','vocab'}, dimensions={0} | all-to-all | bytes 131072 | tf_op jit(solution)/shard_map/norm/all_to_all | solution.py:215
  85.0 0.0 copy-done.1
  85.0 0.0 copy-done.2
  85.0 0.0 copy-done
  85.0 4.0 %adam.1 = (bf16[256,5376]{1,0:T(8,128)(2,1)}, bf16[256,5376]{1,0:T(8,128)(2,1)}, bf16[256,5376]{1,0:T(8,128)(2,1)}) custom-call(f32[128,128]{1,0:T(8,128)S(1)} %bitcast.10, f32[256,5376]{1,0:T(8,128)S(1)} %get-tuple-element.6.refs_1_, bf16[256,5376]{1,0:T(8,128)(2,1)S(1)} %copy-done, bf16[256,5376]{1,0:T(8,128)(2,1)S(1)} %copy-done.1, ...), custom_call_target="tpu_custom_call" | custom-call | tf_op jit(solution)/shard_map/adam/pallas_call | solution.py:219
Async XLA Ops:
  4.1 80.9 %copy-start.1 = (bf16[256,5376]{1,0:T(8,128)(2,1)S(1)}, bf16[256,5376]{1,0:T(8,128)(2,1)}, u32[]{:S(2)}) copy-start(bf16[256,5376]{1,0:T(8,128)(2,1)} %refs_3_.1) | copy-start | bytes 8257540
  4.1 80.8 %copy-start.2 = (bf16[256,5376]{1,0:T(8,128)(2,1)S(1)}, bf16[256,5376]{1,0:T(8,128)(2,1)}, u32[]{:S(2)}) copy-start(bf16[256,5376]{1,0:T(8,128)(2,1)} %refs_4_.1) | copy-start | bytes 8257540
  68.9 16.1 %copy-start = (bf16[256,5376]{1,0:T(8,128)(2,1)S(1)}, bf16[256,5376]{1,0:T(8,128)(2,1)}, u32[]{:S(2)}) copy-start(bf16[256,5376]{1,0:T(8,128)(2,1)} %refs_2_.3) | copy-start | bytes 8257540
